TPU v7x, 32 devices: a whole 2x2x4 slice. The times are simulated.
32 devices in a mesh: tok: 2 (over x), dict: 16 (over z, y, core).
Axes of the slice: x: 2, y: 2, z: 4, core: 2. Of those that a mesh axis runs over, the one named last changes fastest.
Arguments:
- inputs: bfloat16 [1024, 4608], P('tok', 'dict'), may hold values from -6 to 6
- target: bfloat16 [1024, 4608], P('tok', 'dict'), may hold values from -6 to 6
- enc_weight: bfloat16 [4608, 2048], P(None, 'dict'), may hold values from -0.09375 to 0.09375
- enc_bias: float32 [2048], P('dict'), may hold values from -3 to 3
- dec_weight: bfloat16 [2048, 4608], P('dict'), may hold values from -0.75 to 0.75
- dec_bias: float32 [4608], P('dict'), may hold values from -3 to 3
- skip_weight: bfloat16 [4608, 4608], P(None, 'dict'), may hold values from -0.09375 to 0.09375
- block_ids: int32 [1024, 4], P('tok'), may hold values from 0 to 127, as said below
- slot_lists: int32 [2, 16, 384], P('tok'), may hold values from 0 to 2047, as said below
- slot_counts: int32 [2, 16], P('tok'), may hold values from 0 to 384, as said below
Outputs:
- grad_enc: float32 [4608, 2048], P('tok', 'dict')
- grad_dec: float32 [2048, 4608], P('dict', 'tok')
- grad_skip: float32 [4608, 4608], P('tok', 'dict')
Inputs may be any that keep to these rules, and one draw needn't show every extreme that they name: `block_ids`: each token names 4 different blocks of 16 latents. `slot_lists`: A valid slot of list (g, o) holds a code index t * 4 + r of group g (its token t, the token's r-th block); every code of a group stands in exactly one valid slot, in the list of the owner of its block; invalid slots hold 0. `slot_counts`: in every group some list is full.
All inputs are finite; a program needn't handle non-finite values.
Results may differ from a plain program's by a relative error of at most 0.012.
Values may be sent and summed in bfloat16 or wider, within the bound.
A program may use at most 64 MiB of HBM per device.

v0:
```python
import math

import jax
import jax.numpy as jnp
from jax import lax
from jax.sharding import PartitionSpec as P

BLK = 16


def gelu_pair(pre):
    factor = math.sqrt(2.0 / math.pi)
    inner = jnp.tanh(factor * (pre + 0.044715 * pre * pre * pre))
    value = 0.5 * pre * (1.0 + inner)
    slope = 0.5 * (1.0 + inner) + 0.5 * pre * (1.0 - inner * inner) * factor * (
        1.0 + 3.0 * 0.044715 * pre * pre
    )
    return (value, slope)


def local(
    inputs,
    target,
    enc_weight,
    enc_bias,
    dec_weight,
    dec_bias,
    skip_weight,
    block_ids,
    slot_lists,
    slot_counts,
):
    tok_rows, feat_dev = inputs.shape
    lat_dev = enc_weight.shape[1]
    capacity = slot_lists.shape[2]
    per_token = block_ids.shape[1]
    owner = lax.axis_index("dict")
    total_tokens = tok_rows * lax.axis_size("tok")
    scale = 1.0 / math.sqrt(total_tokens)
    whole = lax.all_gather(inputs, "dict", axis=1, tiled=True)
    slots_all = slot_lists[0]
    counts_all = slot_counts[0]
    valid_all = jnp.arange(capacity, dtype=jnp.int32)[None, :] < counts_all[:, None]
    rows_all = (slots_all // per_token).reshape(-1)
    my_slots = lax.dynamic_index_in_dim(slots_all, owner, 0, keepdims=False)
    my_valid = lax.dynamic_index_in_dim(valid_all, owner, 0, keepdims=False)
    my_rows = my_slots // per_token
    my_blocks = block_ids.reshape(-1)[my_slots]
    latent = owner * lat_dev + jnp.arange(lat_dev, dtype=jnp.int32)
    active = (latent[None, :] // BLK == my_blocks[:, None]) & my_valid[:, None]
    picked = whole[my_rows]
    pre = jnp.dot(picked, enc_weight, preferred_element_type=jnp.float32) + enc_bias[None, :]
    value, slope = gelu_pair(pre)
    code = jnp.where(active, value, 0.0).astype(jnp.bfloat16)
    decoded = jnp.dot(code, dec_weight, preferred_element_type=jnp.float32).astype(jnp.bfloat16)
    arrived = lax.all_to_all(decoded, "dict", split_axis=1, concat_axis=0, tiled=True)
    placed = jnp.where(valid_all.reshape(-1)[:, None], arrived.astype(jnp.float32), 0.0)
    recon = jnp.zeros((tok_rows, feat_dev), jnp.float32).at[rows_all].add(placed)
    skip = jnp.dot(whole, skip_weight, preferred_element_type=jnp.float32)
    err = recon + skip + dec_bias[None, :] - target.astype(jnp.float32)
    grad_out = (err * scale).astype(jnp.bfloat16)
    full_grad = lax.all_gather(grad_out, "dict", axis=1, tiled=True)
    grad_rows = full_grad[my_rows]
    back = lax.dot_general(
        grad_rows, dec_weight, (((1,), (1,)), ((), ())), preferred_element_type=jnp.float32
    )
    dpre = jnp.where(active, back * slope, 0.0).astype(jnp.bfloat16)
    enc_term = lax.dot_general(
        picked, dpre, (((0,), (0,)), ((), ())), preferred_element_type=jnp.float32
    )
    dec_term = lax.dot_general(
        code, grad_rows, (((0,), (0,)), ((), ())), preferred_element_type=jnp.float32
    )
    skip_term = lax.dot_general(
        whole, grad_out, (((0,), (0,)), ((), ())), preferred_element_type=jnp.float32
    )
    grad_enc, grad_dec, grad_skip = (
        lax.psum_scatter(
            enc_term.astype(jnp.bfloat16), "tok", scatter_dimension=0, tiled=True
        ).astype(jnp.float32),
        lax.psum_scatter(
            dec_term.astype(jnp.bfloat16), "tok", scatter_dimension=1, tiled=True
        ).astype(jnp.float32),
        lax.psum_scatter(
            skip_term.astype(jnp.bfloat16), "tok", scatter_dimension=0, tiled=True
        ).astype(jnp.float32),
    )
    return (grad_enc, grad_dec, grad_skip)


def solution(mesh):
    in_specs = (
        P("tok", "dict"),
        P("tok", "dict"),
        P(None, "dict"),
        P("dict"),
        P("dict", None),
        P("dict"),
        P(None, "dict"),
        P("tok", None),
        P("tok", None, None),
        P("tok", None),
    )
    out_specs = (P("tok", "dict"), P("dict", "tok"), P("tok", "dict"))
    return jax.shard_map(local, mesh=mesh, in_specs=in_specs, out_specs=out_specs, check_vma=False)
```

profile of v0, /device:TPU:0, one launch (start us, length us, event | category | flops | bytes accessed | tf_op | source)
XLA Modules:
  0.0 389.6 jit_solution(17805692864841842089)
XLA Ops:
  7.9 0.9 copy.29
  9.0 0.7 fusion.26
  9.7 2.5 gather_fusion.1
  13.1 53.3 %all-gather.3.cloned.1.call-done = bf16[512,4608]{0,1:T(8,128)(2,1)} async-done(((bf16[512,288]{0,1:T(8,128)(2,1)}), bf16[512,4608]{0,1:T(8,128)(2,1)}) %all-gather.3.cloned.1.call-update) | async-done | bytes 4718608 | tf_op jit(solution)/shard_map/all_gather | solution.py:40
  66.4 6.7 %copy.28 = bf16[512,4608]{1,0:T(8,128)(2,1)} copy(bf16[512,4608]{0,1:T(8,128)(2,1)} %all-gather.3.cloned.1.call-done) | data formatting | bytes 9437184 | tf_op jit(solution)/shard_map/all_gather | solution.py:40
  73.1 12.2 %gather_fusion = bf16[384,4608]{1,0:T(8,128)(2,1)} fusion(bf16[512,4608]{1,0:T(8,128)(2,1)} %copy.28, s32[1024]{0:T(1024)S(1)} %get-tuple-element.6), kind=kCustom, calls=%fused_computation | custom fusion | bytes 7079424 | tf_op jit(solution)/shard_map/gather | solution.py:51
  85.3 3.5 convolution_add_fusion.1
  88.9 2.9 convolution_convert_fusion
  91.8 5.7 %copy.30 = bf16[384,4608]{0,1:T(8,128)(2,1)} copy(bf16[384,4608]{1,0:T(8,128)(2,1)} %convolution_convert_fusion) | data formatting | bytes 7077888 | tf_op jit(solution)/shard_map/convert_element_type | solution.py:55
  97.6 4.6 %all-to-all-start = ((bf16[384,16,288]{0,2,1:T(8,128)(2,1)}), bf16[384,16,288]{0,2,1:T(8,128)(2,1)}, u32[]{:S(2)}, u32[]{:S(2)}) async-start(bf16[384,16,288]{0,2,1:T(8,128)(2,1)} %bitcast.35), calls=%async_computation | async-start | bytes 7077888 | tf_op jit(solution)/shard_map/all_to_all | solution.py:56
  103.3 0.9 compare_select_fusion
  104.2 4.7 %convolution_add_fusion = f32[512,288]{0,1:T(8,128)} fusion(bf16[4608,288]{0,1:T(8,128)(2,1)S(1)} %copy-done, bf16[512,4608]{0,1:T(8,128)(2,1)} %all-gather.3.cloned.1.call-done, f32[288]{0:T(512)} %param.15), kind=kOutput, calls=%fused_computation.11 | convolution fusion | flops 1359101952 | bytes 7963776 | tf_op jit(solution)/shard_map/dot_general | solution.py:59
  108.9 1.3 copy.32
  110.2 58.2 %all-to-all-done = bf16[384,16,288]{0,2,1:T(8,128)(2,1)} async-done(((bf16[384,16,288]{0,2,1:T(8,128)(2,1)}), bf16[384,16,288]{0,2,1:T(8,128)(2,1)}, u32[]{:S(2)}, u32[]{:S(2)}) %all-to-all-start) | async-done | bytes 3538976 | tf_op jit(solution)/shard_map/all_to_all | solution.py:56
  168.4 2.7 convert_bitcast_fusion
  171.1 0.9 copy.37
  172.0 3.4 broadcast_select_fusion
  175.4 8.9 %copy.33 = f32[6144,288]{1,0:T(8,128)} copy(f32[6144,288]{0,1:T(8,128)} %broadcast_select_fusion) | data formatting | bytes 14155776 | tf_op jit(solution)/shard_map/jit(_where)/select_n | solution.py:57
  184.3 41.5 %scatter_fusion = f32[512,288]{1,0:T(8,128)S(1)} fusion(f32[512,288]{1,0:T(8,128)S(1)} %copy.32, s32[6144]{0:T(1024)S(1)} %bitcast.37, f32[6144,288]{1,0:T(8,128)} %copy.33), kind=kCustom, calls=%fused_computation.3 | custom fusion | flops 1769472 | bytes 21258240 | tf_op jit(solution)/shard_map/scatter-add | solution.py:58
  225.8 0.9 copy.35
  226.8 6.0 %fusion = bf16[4608,288]{0,1:T(8,128)(2,1)} fusion(bf16[512,288]{1,0:T(8,128)(2,1)S(1)} %multiply_convert_fusion, bf16[512,4608]{0,1:T(8,128)(2,1)} %all-gather.3.cloned.1.call-done), kind=kOutput, calls=%fused_computation.7 | convolution fusion | flops 1360281600 | bytes 7667712 | tf_op jit(solution)/shard_map/dot_general | solution.py:74
  233.1 59.4 %all-gather.5.cloned.1.call-done = bf16[512,4608]{0,1:T(8,128)(2,1)} async-done(((bf16[512,288]{0,1:T(8,128)(2,1)}), bf16[512,4608]{0,1:T(8,128)(2,1)}) %all-gather.5.cloned.1.call-update) | async-done | bytes 4718608 | tf_op jit(solution)/shard_map/all_gather | solution.py:62
  292.5 6.7 %copy.36 = bf16[512,4608]{1,0:T(8,128)(2,1)} copy(bf16[512,4608]{0,1:T(8,128)(2,1)} %all-gather.5.cloned.1.call-done) | data formatting | bytes 9437184 | tf_op jit(solution)/shard_map/all_gather | solution.py:62
  299.2 12.9 %gather_fusion.2 = bf16[384,4608]{1,0:T(8,128)(2,1)} fusion(bf16[512,4608]{1,0:T(8,128)(2,1)} %copy.36, s32[1024]{0:T(1024)S(1)} %copy-done.7), kind=kCustom, calls=%fused_computation.2 | custom fusion | bytes 7079424 | tf_op jit(solution)/shard_map/gather | solution.py:63
  312.1 4.0 %convolution_convert_fusion.2 = bf16[128,4608]{1,0:T(8,128)(2,1)} fusion(bf16[384,4608]{1,0:T(8,128)(2,1)} %gather_fusion.2, f32[384,128]{1,0:T(8,128)S(1)} %convolution_add_fusion.1, s32[128]{0:T(128)S(1)} %copy-done.10, s32[384]{0:T(512)S(1)} %gather_fusion.1, pred[384]{0:T(512)(128)(4,1)S(1)} %dynamic-slice_reduce_fusion), kind=kOutput, calls=%fused_computation.8 | convolution fusion | flops 454164480 | bytes 4917632 | tf_op jit(solution)/shard_map/dot_general | solution.py:71
  316.2 8.1 %convolution_convert_fusion.3 = bf16[4608,128]{1,0:T(8,128)(2,1)} fusion(bf16[384,4608]{1,0:T(8,128)(2,1)} %gather_fusion, bf16[384,4608]{1,0:T(8,128)(2,1)} %gather_fusion.2, bf16[128,4608]{1,0:T(8,128)(2,1)S(1)} %copy-done.3, f32[384,128]{1,0:T(8,128)S(1)} %convolution_add_fusion.1, s32[128]{0:T(128)S(1)} %copy-done.10, s32[384]{0:T(512)S(1)} %gather_fusion.1, ...), kind=kOutput, calls=%fused_computation.9 | convolution fusion | flops 907640832 | bytes 9636224 | tf_op jit(solution)/shard_map/dot_general | solution.py:68
  324.4 7.5 %reduce-scatter.8.cloned.1.call-done = bf16[2304,288]{0,1:T(8,128)(2,1)} async-done(((bf16[4608,288]{0,1:T(8,128)(2,1)}), bf16[2304,288]{0,1:T(8,128)(2,1)}) %reduce-scatter.8.cloned.1.call-update) | async-done | bytes 1327120 | tf_op jit(solution)/shard_map/reduce_scatter | solution.py:84
  331.9 3.0 convert_element_type.59
  334.9 21.5 %reduce-scatter.6.cloned.1.call-done = bf16[128,2304]{1,0:T(8,128)(2,1)} async-done(((bf16[128,4608]{1,0:T(8,128)(2,1)}), bf16[128,2304]{1,0:T(8,128)(2,1)}) %reduce-scatter.6.cloned.1.call-update) | async-done | bytes 589840 | tf_op jit(solution)/shard_map/reduce_scatter | solution.py:81
  356.3 2.2 convert_element_type.56
  358.5 22.4 %reduce-scatter.4.cloned.1.call-done = bf16[2304,128]{1,0:T(8,128)(2,1)} async-done(((bf16[4608,128]{1,0:T(8,128)(2,1)}), bf16[2304,128]{1,0:T(8,128)(2,1)}) %reduce-scatter.4.cloned.1.call-update) | async-done | bytes 589840 | tf_op jit(solution)/shard_map/reduce_scatter | solution.py:78
  380.9 2.2 convert_element_type.54
  (41 shorter events, 3.3 us)
Async XLA Ops:
  7.2 97.0 %copy-start = (bf16[4608,288]{0,1:T(8,128)(2,1)S(1)}, bf16[4608,288]{0,1:T(8,128)(2,1)}, u32[]{:S(2)}) copy-start(bf16[4608,288]{0,1:T(8,128)(2,1)} %param.16) | copy-start | bytes 7962628
  7.2 59.2 %all-gather.3.cloned.1.call-start = ((), (), s32[]{:S(2)}) async-start(), calls=%async_computation.4 | async-start | bytes 5013504 | tf_op jit(solution)/shard_map/all_gather | solution.py:40
  9.7 63.4 %copy-start.6 = (s32[1024]{0:T(1024)}, s32[1024]{0:T(1024)S(1)}, u32[]{:S(2)}) copy-start(s32[1024]{0:T(1024)S(1)} %get-tuple-element.6) | copy-start | bytes 12292
  13.1 75.8 %copy-start.9 = (s32[128]{0:T(128)}, s32[128]{0:T(128)S(1)}, u32[]{:S(2)}) copy-start(s32[128]{0:T(128)S(1)} %and_select_fusion.2) | copy-start | bytes 1540
  73.1 12.2 %copy-start.8 = (f32[128]{0:T(128)S(1)}, f32[128]{0:T(128)}, u32[]{:S(2)}) copy-start(f32[128]{0:T(128)} %param.13) | copy-start | bytes 1540
  85.3 3.5 copy-start.2
  97.5 4.9 %copy-start.5 = (s32[1,16,384]{2,1,0:T(8,128)S(1)}, s32[1,16,384]{2,1,0:T(8,128)}, u32[]{:S(2)}) copy-start(s32[1,16,384]{2,1,0:T(8,128)} %param.18) | copy-start | bytes 73732
  97.6 5.5 %copy-start.4 = (bf16[512,288]{0,1:T(8,128)(2,1)S(1)}, bf16[512,288]{0,1:T(8,128)(2,1)}, u32[]{:S(2)}) copy-start(bf16[512,288]{0,1:T(8,128)(2,1)} %param.11) | copy-start | bytes 884740
  97.6 70.8 %all-to-all-start = ((bf16[384,16,288]{0,2,1:T(8,128)(2,1)}), bf16[384,16,288]{0,2,1:T(8,128)(2,1)}, u32[]{:S(2)}, u32[]{:S(2)}) async-start(bf16[384,16,288]{0,2,1:T(8,128)(2,1)} %bitcast.35), calls=%async_computation | async-start | bytes 7077888 | tf_op jit(solution)/shard_map/all_to_all | solution.py:56
  102.2 190.3 %all-gather.5.cloned.1.call-start = ((), (), s32[]{:S(2)}) async-start(), calls=%async_computation.5 | async-start | bytes 5013504 | tf_op jit(solution)/shard_map/all_gather | solution.py:62
  226.7 105.1 %reduce-scatter.8.cloned.1.call-start = ((), (), s32[]{:S(2)}) async-start(), calls=%async_computation.8 | async-start | bytes 3981312 | tf_op jit(solution)/shard_map/reduce_scatter | solution.py:84
  232.8 66.5 %copy-start.7 = (s32[1024]{0:T(1024)S(1)}, s32[1024]{0:T(1024)}, u32[]{:S(2)}) copy-start(s32[1024]{0:T(1024)} %copy-done.6) | copy-start | bytes 12292
  232.8 123.5 %reduce-scatter.6.cloned.1.call-start = ((), (), s32[]{:S(2)}) async-start(), calls=%async_computation.7 | async-start | bytes 1769472 | tf_op jit(solution)/shard_map/reduce_scatter | solution.py:81
  299.2 12.9 %copy-start.10 = (s32[128]{0:T(128)S(1)}, s32[128]{0:T(128)}, u32[]{:S(2)}) copy-start(s32[128]{0:T(128)} %copy-done.9) | copy-start | bytes 1540
  312.1 4.1 %copy-start.3 = (bf16[128,4608]{1,0:T(8,128)(2,1)S(1)}, bf16[128,4608]{1,0:T(8,128)(2,1)}, u32[]{:S(2)}) copy-start(bf16[128,4608]{1,0:T(8,128)(2,1)} %param.14) | copy-start | bytes 3538948
  316.2 64.7 %reduce-scatter.4.cloned.1.call-start = ((), (), s32[]{:S(2)}) async-start(), calls=%async_computation.6 | async-start | bytes 1769472 | tf_op jit(solution)/shard_map/reduce_scatter | solution.py:78
  324.4 58.7 %copy-start.1 = (bf16[4608,288]{0,1:T(8,128)(2,1)S(1)}, bf16[4608,288]{0,1:T(8,128)(2,1)}, u32[]{:S(2)}) copy-start(bf16[4608,288]{0,1:T(8,128)(2,1)} %param.16) | copy-start | bytes 7962628
Sparse Core Ops, SparseCore 0:
  10.3 56.0 all-gather.2
  226.9 65.6 all-gather.4
  295.3 36.4 reduce-scatter.7
  334.6 21.7 reduce-scatter.5
  359.1 21.7 reduce-scatter.3
where the time goes:
time: 391 us; the launch traced here: 390 us
  waiting for transfers between devices  223 us (57%)
  local copies, waits for them, and re-layouts  60.7 us (16%)
  other arithmetic  57.3 us (15%)
  matrix products  29.3 us (7%)
  between operations  14 us (4%)
  starting transfers between devices  5.24 us (1%)
    all_gather x1, waiting for transfers between devices, local(): full_grad = lax.all_gather(grad_out, 'dict', axis=1, tiled=True)  59.4 us
    all_to_all x1, waiting for transfers between devices, local(): lax.all_to_all(decoded, 'dict', split_axis=1, concat_axis=0, tiled=True)  58.2 us
    all_gather x1, waiting for transfers between devices, local(): whole = lax.all_gather(inputs, 'dict', axis=1, tiled=True)  53.3 us
    scatter-add x1, other arithmetic, local(): jnp.zeros((tok_rows, feat_dev), jnp.float32).at[rows_all].add(placed)  41.5 us
    reduce_scatter x1, waiting for transfers between devices, local(): lax.psum_scatter(enc_term.astype(jnp.bfloat16), 'tok', scatter_dimension=...  22.4 us
    reduce_scatter x1, waiting for transfers between devices, local(): lax.psum_scatter(dec_term.astype(jnp.bfloat16), 'tok', scatter_dimension=...  21.5 us
    gather x1, local copies, waits for them, and re-layouts, local(): grad_rows = full_grad[my_rows]  12.9 us
    gather x1, local copies, waits for them, and re-layouts, local(): picked = whole[my_rows]  12.2 us
  transfers between devices with their start and end apart: 6, of which 6 were waited for; matrix products, arithmetic and copies ran while one was open for 14% of the time, Pallas kernels for 0%

commit v1 on v0

v1 whole, which is shorter than its diff:
```python
import math

import jax
import jax.numpy as jnp
from jax import lax
from jax.sharding import PartitionSpec as P

BLK = 16


def gelu_pair(pre):
    factor = math.sqrt(2.0 / math.pi)
    inner = jnp.tanh(factor * (pre + 0.044715 * pre * pre * pre))
    value = 0.5 * pre * (1.0 + inner)
    slope = 0.5 * (1.0 + inner) + 0.5 * pre * (1.0 - inner * inner) * factor * (
        1.0 + 3.0 * 0.044715 * pre * pre
    )
    return (value, slope)


def local(
    inputs,
    target,
    enc_weight,
    enc_bias,
    dec_weight,
    dec_bias,
    skip_weight,
    block_ids,
    slot_lists,
    slot_counts,
):
    tok_rows, feat_dev = inputs.shape
    feat, lat_dev = enc_weight.shape
    owner = lax.axis_index("dict")
    n_dict = lax.axis_size("dict")
    n_tok = lax.axis_size("tok")
    scale = 1.0 / math.sqrt(tok_rows * n_tok)
    f32, bf16 = jnp.float32, jnp.bfloat16
    blocks = (owner * lat_dev + jnp.arange(lat_dev, dtype=jnp.int32)) // BLK
    active = jnp.any(block_ids[:, :, None] == blocks[None, None, :], axis=1)
    whole = lax.all_gather(inputs, "dict")
    dec_cols = lax.all_to_all(
        dec_weight.reshape(lat_dev, n_dict, feat_dev), "dict", split_axis=1, concat_axis=0, tiled=True
    ).reshape(n_dict * lat_dev, feat_dev)
    enc_blocks = enc_weight.reshape(n_dict, feat_dev, lat_dev)
    pre = jnp.einsum("btf,bfl->tl", whole, enc_blocks, preferred_element_type=f32) + enc_bias[None, :]
    value, slope = gelu_pair(pre)
    code = jnp.where(active, value, 0.0).astype(bf16)
    codes = lax.all_gather(code, "dict", axis=1, tiled=True)
    skip = jnp.einsum(
        "btf,bfm->tm", whole, skip_weight.reshape(n_dict, feat_dev, feat_dev), preferred_element_type=f32
    )
    recon = jnp.dot(codes, dec_cols, preferred_element_type=f32)
    err = recon + skip + dec_bias[None, :] - target.astype(f32)
    grad_out = (err * scale).astype(bf16)
    back = lax.dot_general(
        dec_cols, grad_out, (((1,), (1,)), ((), ())), preferred_element_type=f32
    ).astype(bf16)
    back = lax.all_to_all(
        back.reshape(n_dict, lat_dev, tok_rows), "dict", split_axis=0, concat_axis=0
    )
    skip_term = jnp.einsum("btf,tm->bfm", whole, grad_out, preferred_element_type=f32)
    skip_term = skip_term.reshape(feat, feat_dev).astype(bf16)
    grad_skip = lax.psum_scatter(skip_term, "tok", scatter_dimension=0, tiled=True).astype(f32)
    dec_term = lax.dot_general(
        codes, grad_out, (((0,), (0,)), ((), ())), preferred_element_type=f32
    ).astype(bf16)
    dec_term = lax.all_to_all(
        dec_term.reshape(n_dict, lat_dev, feat_dev), "dict", split_axis=0, concat_axis=0
    )
    dec_term = lax.psum_scatter(dec_term, "tok", scatter_dimension=0, tiled=True)
    grad_dec = dec_term.transpose(1, 0, 2).reshape(lat_dev, feat // n_tok).astype(f32)
    total = jnp.sum(back.astype(f32), axis=0).T
    dpre = jnp.where(active, total * slope, 0.0).astype(bf16)
    enc_term = jnp.einsum("btf,tl->bfl", whole, dpre, preferred_element_type=f32)
    enc_term = enc_term.reshape(feat, lat_dev).astype(bf16)
    grad_enc = lax.psum_scatter(enc_term, "tok", scatter_dimension=0, tiled=True).astype(f32)
    return (grad_enc, grad_dec, grad_skip)


def solution(mesh):
    in_specs = (
        P("tok", "dict"),
        P("tok", "dict"),
        P(None, "dict"),
        P("dict"),
        P("dict", None),
        P("dict"),
        P(None, "dict"),
        P("tok", None),
        P("tok", None, None),
        P("tok", None),
    )
    out_specs = (P("tok", "dict"), P("dict", "tok"), P("tok", "dict"))
    return jax.shard_map(local, mesh=mesh, in_specs=in_specs, out_specs=out_specs, check_vma=False)
```

time: 391 us -> 265 us (0.68)
  waiting for transfers between devices: 223 us -> 104 us
  blocking collectives: 0 us -> 83.6 us
  other arithmetic: 57.3 us -> 7.65 us
  local copies, waits for them, and re-layouts: 60.7 us -> 28.6 us
  matrix products: 29.3 us -> 22.5 us
    all_to_all x0 -> x2, blocking collectives: none -> 83.6 us  [the longest x1 50.5 us: local(): lax.all_to_all(back.reshape(n_dict, lat_dev, tok_rows), 'dict', split_axi...]
    all_to_all x1, waiting for transfers between devices: 58.2 us -> 14.4 us  [local(): lax.all_to_all(dec_weight.reshape(lat_dev, n_dict, feat_dev), 'dict', spl...]
    scatter-add x1 -> x0, other arithmetic: 41.5 us -> none  [local(): jnp.zeros((tok_rows, feat_dev), jnp.float32).at[rows_all].add(placed)]
    all_gather x2, waiting for transfers between devices: 113 us -> 72 us  [the longest x1 59.9 us: local(): whole = lax.all_gather(inputs, 'dict')]
    reduce_scatter x3, waiting for transfers between devices: 51.3 us -> 16.8 us  [the longest x1 16.7 us: local(): lax.psum_scatter(enc_term, 'tok', scatter_dimension=0, tiled=True)]
    gather x3 -> x0, local copies, waits for them, and re-layouts: 27.6 us -> none  [the longest x1 12.9 us: local(): grad_rows = full_grad[my_rows]]
    reshape x1 -> x4, local copies, waits for them, and re-layouts: 0.16 us -> 15.5 us  [the longest x2 14.7 us: local(): skip_weight.reshape(n_dict, feat_dev, feat_dev)]
    all_gather x2 -> x0, local copies, waits for them, and re-layouts: 13.5 us -> none  [the longest x1 6.73 us: local(): full_grad = lax.all_gather(grad_out, 'dict', axis=1, tiled=True)]
  transfers between devices with their start and end apart: 6 -> 6, of which waited for: 6 -> 4; matrix products, arithmetic and copies ran while one was open for 14% -> 17% of each run, Pallas kernels for 0% -> 0%
where the time goes in v1:
time: 265 us; the launch traced here: 264 us
  waiting for transfers between devices  104 us (39%)
  blocking collectives  83.6 us (32%)
  local copies, waits for them, and re-layouts  28.6 us (11%)
  matrix products  22.5 us (8%)
  between operations  14 us (5%)
  other arithmetic  7.65 us (3%)
  starting transfers between devices  4.08 us (2%)
    all_gather x1, waiting for transfers between devices, local(): whole = lax.all_gather(inputs, 'dict')  59.9 us
    all_to_all x1, blocking collectives, local(): lax.all_to_all(back.reshape(n_dict, lat_dev, tok_rows), 'dict', split_axi...  50.5 us
    all_to_all x1, blocking collectives, local(): lax.all_to_all(dec_term.reshape(n_dict, lat_dev, feat_dev), 'dict', split...  33 us
    reduce_scatter x1, waiting for transfers between devices, local(): lax.psum_scatter(enc_term, 'tok', scatter_dimension=0, tiled=True)  16.7 us
    reshape x2, local copies, waits for them, and re-layouts, local(): skip_weight.reshape(n_dict, feat_dev, feat_dev)  14.7 us
    all_to_all x1, waiting for transfers between devices, local(): lax.all_to_all(dec_weight.reshape(lat_dev, n_dict, feat_dev), 'dict', spl...  14.4 us
    all_gather x1, waiting for transfers between devices, local(): codes = lax.all_gather(code, 'dict', axis=1, tiled=True)  12.1 us
    unnamed x27, local copies, waits for them, and re-layouts  8 us
  transfers between devices with their start and end apart: 6, of which 4 were waited for; matrix products, arithmetic and copies ran while one was open for 17% of the time, Pallas kernels for 0%

profile of v1, /device:TPU:0, one launch (start us, length us, event | category | flops | bytes accessed | tf_op | source)
XLA Modules:
  0.0 264.3 jit_solution(3209855116896849321)
XLA Ops:
  7.2 0.7 all-gather.6.cloned.1.call-update
  8.0 1.1 compare_reduce_fusion
  9.1 59.9 %all-gather.6.cloned.1.call-done = bf16[8192,288]{0,1:T(8,128)(2,1)} async-done(((bf16[512,288]{0,1:T(8,128)(2,1)}), bf16[8192,288]{0,1:T(8,128)(2,1)}) %all-gather.6.cloned.1.call-update) | async-done | bytes 4718608 | tf_op jit(solution)/shard_map/all_gather | solution.py:42
  68.9 4.5 %copy.50 = bf16[36,8,16,512]{3,2,1,0:T(8,128)(2,1)S(1)} copy(bf16[36,8,16,512]{3,1,2,0:T(8,128)(2,1)} %bitcast.76) | data formatting | bytes 9437184
  73.4 2.3 select_convert_fusion
  75.8 1.4 copy.38
  77.2 3.7 %all-to-all-start = ((bf16[128,16,288]{0,2,1:T(8,128)(2,1)}), bf16[128,16,288]{0,2,1:T(8,128)(2,1)S(1)}, u32[]{:S(2)}, u32[]{:S(2)}) async-start(bf16[128,16,288]{0,2,1:T(8,128)(2,1)} %bitcast.2), calls=%async_computation | async-start | bytes 2359296 | tf_op jit(solution)/shard_map/all_to_all | solution.py:43
  80.9 7.5 %reshape.57 = bf16[16,288,288]{1,0,2:T(8,128)(2,1)} reshape(bf16[4608,288]{0,1:T(8,128)(2,1)} %param.16) | data formatting | bytes 5308416 | tf_op jit(solution)/shard_map/reshape | solution.py:52
  88.5 7.2 %copy.40 = bf16[16,288,288]{2,0,1:T(8,128)(2,1)} copy(bf16[16,288,288]{1,0,2:T(8,128)(2,1)} %reshape.57) | data formatting | bytes 5308416 | tf_op jit(solution)/shard_map/reshape | solution.py:52
  95.7 14.4 %all-to-all-done = bf16[128,16,288]{0,2,1:T(8,128)(2,1)S(1)} async-done(((bf16[128,16,288]{0,2,1:T(8,128)(2,1)}), bf16[128,16,288]{0,2,1:T(8,128)(2,1)S(1)}, u32[]{:S(2)}, u32[]{:S(2)}) %all-to-all-start) | async-done | bytes 1179680 | tf_op jit(solution)/shard_map/all_to_all | solution.py:43
  110.1 0.5 copy.39
  110.6 6.2 %convolution_bitcast_fusion = f32[512,288]{0,1:T(8,128)} fusion(bf16[16,512,288]{1,0,2:T(8,128)(2,1)} %bitcast.82, bf16[16,288,288]{2,0,1:T(8,128)(2,1)} %copy.40), kind=kOutput, calls=%fused_computation.16 | convolution fusion | flops 1358954496 | bytes 7962624 | tf_op jit(solution)/shard_map/btf,bfm->tm/dot_general | solution.py:51
  116.7 12.1 %all-gather.4.cloned.1.call-done = bf16[512,2048]{1,0:T(8,128)(2,1)} async-done(((bf16[512,128]{1,0:T(8,128)(2,1)}), bf16[512,2048]{1,0:T(8,128)(2,1)}) %all-gather.4.cloned.1.call-update) | async-done | bytes 2097168 | tf_op jit(solution)/shard_map/all_gather | solution.py:50
  128.9 2.7 %fusion.17 = bf16[512,288]{0,1:T(8,128)(2,1)S(1)} fusion(f32[512,288]{0,1:T(8,128)} %convolution_bitcast_fusion, bf16[512,2048]{1,0:T(8,128)(2,1)} %all-gather.4.cloned.1.call-done, bf16[36,8,16,128]{3,2,1,0:T(8,128)(2,1)S(1)} %bitcast.87, bf16[512,288]{0,1:T(8,128)(2,1)S(1)} %copy-done.6, f32[288]{0:T(512)S(1)} %copy-done.7), kind=kOutput, calls=%fused_computation.19 | convolution fusion | flops 604864512 | bytes 4457600 | tf_op jit(solution)/shard_map/dot_general | solution.py:54
  131.6 0.8 fusion.13
  132.4 0.2 copy.83
  132.6 33.0 %all_to_all.25 = bf16[16,128,288]{1,2,0:T(8,128)(2,1)} all-to-all(bf16[16,128,288]{1,2,0:T(8,128)(2,1)S(1)} %bitcast.84), channel_id=1, replica_groups=mesh['tok'=2,'dict'=16] {'dict'}, dimensions={0} | all-to-all | bytes 2359296 | tf_op jit(solution)/shard_map/all_to_all | solution.py:69
  165.6 0.2 reduce-scatter.8.cloned.1.call-start
  165.9 6.8 %fusion.6 = bf16[288,16,288]{0,2,1:T(8,128)(2,1)} fusion(bf16[36,16,8,512]{3,2,1,0:T(8,128)(2,1)} %bitcast.77, bf16[512,288]{0,1:T(8,128)(2,1)S(1)} %fusion.17), kind=kOutput, calls=%fused_computation.9 | convolution fusion | flops 1360281600 | bytes 7667712 | tf_op jit(solution)/shard_map/btf,tm->bfm/dot_general | solution.py:63
  172.6 4.6 %copy.45 = bf16[4608,288]{0,1:T(8,128)(2,1)} copy(bf16[4608,288]{1,0:T(8,128)(2,1)} %bitcast.86) | data formatting | bytes 5308416 | tf_op jit(solution)/shard_map/convert_element_type | solution.py:64
  177.3 1.3 fusion.9
  178.7 0.5 copy.82
  179.2 50.5 %all_to_all.26 = bf16[16,128,512]{1,2,0:T(8,128)(2,1)S(1)} all-to-all(bf16[16,128,512]{1,2,0:T(8,128)(2,1)S(1)} %bitcast.75), channel_id=1, replica_groups=mesh['tok'=2,'dict'=16] {'dict'}, dimensions={0} | all-to-all | bytes 4194304 | tf_op jit(solution)/shard_map/all_to_all | solution.py:60
  229.7 0.3 convert_reduce_fusion
  230.1 0.5 copy-done.4
  230.6 0.1 copy-done.9
  230.7 2.6 fusion.10
  233.3 1.1 convert_element_type.77
  234.5 1.4 copy.46
  235.9 3.0 %convert_element_type.75 = f32[2304,288]{0,1:T(8,128)} convert(bf16[2304,288]{0,1:T(8,128)(2,1)} %reduce-scatter.8.cloned.1.call-done) | non-fusion elementwise | flops 663552 | bytes 3981312 | tf_op jit(solution)/shard_map/convert_element_type | solution.py:65
  238.9 16.7 %reduce-scatter.4.cloned.1.call-done = bf16[2304,128]{1,0:T(8,128)(2,1)} async-done(((bf16[4608,128]{1,0:T(8,128)(2,1)}), bf16[2304,128]{1,0:T(8,128)(2,1)}) %reduce-scatter.4.cloned.1.call-update) | async-done | bytes 589840 | tf_op jit(solution)/shard_map/reduce_scatter | solution.py:78
  255.6 2.2 convert_element_type.67
  (34 shorter events, 0.3 us)
Async XLA Ops:
  7.2 66.2 %copy-start = (bf16[4608,128]{1,0:T(8,128)(2,1)S(1)}, bf16[4608,128]{1,0:T(8,128)(2,1)}, u32[]{:S(2)}) copy-start(bf16[4608,128]{1,0:T(8,128)(2,1)} %param.12) | copy-start | bytes 3538948
  7.2 61.7 %all-gather.6.cloned.1.call-start = ((), (), s32[]{:S(2)}) async-start(), calls=%async_computation.10 | async-start | bytes 5013504 | tf_op jit(solution)/shard_map/all_gather | solution.py:42
  7.9 120.9 %all-gather.4.cloned.1.call-start = ((), (), s32[]{:S(2)}) async-start(), calls=%async_computation.6 | async-start | bytes 2228224 | tf_op jit(solution)/shard_map/all_gather | solution.py:50
  9.0 64.4 %copy-start.3 = (pred[512,128]{1,0:T(8,128)(4,1)}, pred[512,128]{1,0:T(8,128)(4,1)S(1)}, u32[]{:S(2)}) copy-start(pred[512,128]{1,0:T(8,128)(4,1)S(1)} %compare_reduce_fusion) | copy-start | bytes 196612
  68.9 4.5 %copy-start.8 = (f32[128]{0:T(128)S(1)}, f32[128]{0:T(128)}, u32[]{:S(2)}) copy-start(f32[128]{0:T(128)} %param.13) | copy-start | bytes 1540
  73.4 2.3 copy-start.1
  73.4 2.3 copy-start.2
  77.2 32.9 %all-to-all-start = ((bf16[128,16,288]{0,2,1:T(8,128)(2,1)}), bf16[128,16,288]{0,2,1:T(8,128)(2,1)S(1)}, u32[]{:S(2)}, u32[]{:S(2)}) async-start(bf16[128,16,288]{0,2,1:T(8,128)(2,1)} %bitcast.2), calls=%async_computation | async-start | bytes 2359296 | tf_op jit(solution)/shard_map/all_to_all | solution.py:43
  80.9 152.4 %reduce-scatter.6.cloned.1.call-start = ((), (), s32[]{:S(2)}) async-start(), calls=%async_computation.8 | async-start | bytes 1769472 | tf_op jit(solution)/shard_map/reduce_scatter | solution.py:72
  110.6 18.3 %copy-start.6 = (bf16[512,288]{0,1:T(8,128)(2,1)S(1)}, bf16[512,288]{0,1:T(8,128)(2,1)}, u32[]{:S(2)}) copy-start(bf16[512,288]{0,1:T(8,128)(2,1)} %param.11) | copy-start | bytes 884740
  110.6 18.3 %copy-start.7 = (f32[288]{0:T(512)S(1)}, f32[288]{0:T(512)}, u32[]{:S(2)}) copy-start(f32[288]{0:T(512)} %param.15) | copy-start | bytes 3460
  128.9 2.7 %copy-start.5 = (bf16[512,2048]{1,0:T(8,128)(2,1)S(1)}, bf16[512,2048]{1,0:T(8,128)(2,1)}, u32[]{:S(2)}) copy-start(bf16[512,2048]{1,0:T(8,128)(2,1)} %all-gather.4.cloned.1.call-done) | copy-start | bytes 6291460
  165.6 70.2 %reduce-scatter.8.cloned.1.call-start = ((), (), s32[]{:S(2)}) async-start(), calls=%async_computation.9 | async-start | bytes 3981312 | tf_op jit(solution)/shard_map/reduce_scatter | solution.py:65
  177.3 78.3 %reduce-scatter.4.cloned.1.call-start = ((), (), s32[]{:S(2)}) async-start(), calls=%async_computation.7 | async-start | bytes 1769472 | tf_op jit(solution)/shard_map/reduce_scatter | solution.py:78
  177.3 52.7 %slice-start = ((s8[4718592]{0:T(1024)(128)(4,1)}), s8[4194304]{0:T(1024)(128)(4,1)S(1)}, s32[]{:S(2)}) async-start(s8[4718592]{0:T(1024)(128)(4,1)} %bitcast.78), calls=%async_computation.11 | async-start | bytes 8388608
  178.6 51.4 %slice-start.1 = ((s8[4718592]{0:T(1024)(128)(4,1)}), s8[524288]{0:T(1024)(128)(4,1)S(1)}, s32[]{:S(2)}) async-start(s8[4718592]{0:T(1024)(128)(4,1)} %bitcast.78), calls=%async_computation.12 | async-start | bytes 1048576
  229.7 0.8 copy-start.4
  229.7 1.0 copy-start.9
Sparse Core Ops, SparseCore 0:
  10.2 58.6 all-gather.5
  75.9 52.9 all-gather.3
  165.8 20.3 reduce-scatter.5
  188.9 37.9 reduce-scatter.7
  233.4 22.1 reduce-scatter.3

commit v2 on v1

--- a/solution.py
+++ b/solution.py
@@ -1,11 +1,15 @@
+import functools
 import math
 
 import jax
 import jax.numpy as jnp
 from jax import lax
+from jax.experimental import pallas as pl
+from jax.experimental.pallas import tpu as pltpu
 from jax.sharding import PartitionSpec as P
 
 BLK = 16
+MESH = pl.DeviceIdType.MESH
 
 
 def gelu_pair(pre):
@@ -16,6 +20,311 @@
         1.0 + 3.0 * 0.044715 * pre * pre
     )
     return (value, slope)
+
+
+def dot(a, b, da, db):
+    return lax.dot_general(a, b, (((da,), (db,)), ((), ())), preferred_element_type=jnp.float32)
+
+
+def fused_kernel(
+    nz, scale,
+    xt, tt, enc, eb, dec, db, sw, ids,
+    ge, gd, gs,
+    encv, decv, swv, x_all, x_oth, dec_t, dec_cols, codes, go_all, go_oth, gd_part, gd_recv,
+    dpre, dpre_oth, skip_acc, pre_acc, slope_s,
+    load_sem, ag_send, ag_recv, xo_send, xo_fwd, xo_recv, dec_send, dec_recv, gd_send, gd_recv_sem,
+    pair_send, pair_recv,
+):
+    f32, bf16 = jnp.float32, jnp.bfloat16
+    n = 4 * nz
+    nh = n // 2
+    t, me = lax.axis_index("tok"), lax.axis_index("dict")
+    z, y, c = me // 4, (me // 2) % 2, me % 2
+    fd, lat = xt.shape[0], enc.shape[1]
+    half = fd // 2
+
+    def at(zz, yy, cc):
+        return (zz * 2 + yy) * 2 + cc
+
+    def rows(i, size):
+        return pl.ds(pl.multiple_of(i * size, 16), size)
+
+    sib, ypeer = (t, at(z, y, 1 - c)), (t, at(z, 1 - y, c))
+    xpeer = (1 - t, me)
+    zs = [(z + k) % nz for k in range(nz)]
+
+    def copy(src, dst, s, r, dev):
+        return pltpu.make_async_remote_copy(
+            src_ref=src, dst_ref=dst, send_sem=s, recv_sem=r, device_id=dev, device_id_type=MESH
+        )
+
+    pending = []
+
+    def send(src, dst, s, r, dev):
+        cp = copy(src, dst, s, r, dev)
+        cp.start()
+        pending.append(cp)
+
+    def arrived(ref, r):
+        copy(ref, ref, pair_send.at[0], r, xpeer).wait_recv()
+
+    def gather_own(p, buf, size):
+        own = buf.at[rows(me, size)]
+        for k in range(1, nz):
+            send(own, own, ag_send.at[p, k - 1], ag_recv.at[p, me], (t, at(zs[k], y, c)))
+        send(own, own, ag_send.at[p, nz - 1], ag_recv.at[p, me], ypeer)
+        send(own, own, ag_send.at[p, nz], ag_recv.at[p, me], sib)
+
+    def gather_z(p, buf, size, extra):
+        extra(me, z)
+        for k in range(1, nz):
+            d = at(zs[nz - k], y, c)
+            blk = buf.at[rows(d, size)]
+            arrived(blk, ag_recv.at[p, d])
+            send(blk, blk, ag_send.at[p, nz + 2 * k - 1], ag_recv.at[p, d], ypeer)
+            send(blk, blk, ag_send.at[p, nz + 2 * k], ag_recv.at[p, d], sib)
+            extra(d, zs[nz - k])
+
+    def gather_y(p, buf, size, extra):
+        for k in range(nz):
+            d = at(zs[(nz - k) % nz], 1 - y, c)
+            blk = buf.at[rows(d, size)]
+            arrived(blk, ag_recv.at[p, d])
+            send(blk, blk, ag_send.at[p, 3 * nz - 1 + k], ag_recv.at[p, d], sib)
+            extra(d, zs[(nz - k) % nz])
+
+    def nothing(d, zz):
+        pass
+
+    barrier = pltpu.get_barrier_semaphore()
+    pl.semaphore_signal(barrier, inc=1, device_id=xpeer, device_id_type=MESH)
+    for k in range(1, n):
+        pl.semaphore_signal(barrier, inc=1, device_id=(t, (me + k) % n), device_id_type=MESH)
+    loads = [
+        pltpu.make_async_copy(s, d, load_sem.at[i])
+        for i, (s, d) in enumerate(((dec, decv), (enc, encv), (sw, swv)))
+    ]
+    for cp in loads:
+        cp.start()
+    x_all[rows(me, fd), :] = xt[...]
+    skip_acc[...] = jnp.zeros_like(skip_acc)
+    pre_acc[...] = jnp.zeros_like(pre_acc)
+    pl.semaphore_wait(barrier, n)
+
+    gather_own(0, x_all, fd)
+    loads[0].wait()
+    width = dec_t.shape[1]
+    for j in range(dec_t.shape[0] // width):
+        dec_t[j * width : (j + 1) * width, :] = decv[:, j * width : (j + 1) * width].T
+
+    def to_other(d, zz):
+        @pl.when(zz // (nz // 2) == 1 - t)
+        def _():
+            j = d % nh
+            copy(
+                x_all.at[rows(d, fd)], x_oth.at[rows(j, fd)], xo_send.at[j], xo_recv.at[j], xpeer
+            ).start()
+
+    gather_z(0, x_all, fd, to_other)
+
+    cols = pl.ds(pl.multiple_of(me * lat, 128), lat)
+    part = pl.ds(pl.multiple_of(t * half, 16), half)
+    for k in range(1, n):
+        d = (me + k) % n
+        send(
+            dec_t.at[pl.ds(pl.multiple_of(d * fd + t * half, 16), half)],
+            dec_cols.at[part, cols],
+            dec_send.at[k - 1],
+            dec_recv.at[me],
+            (t, d),
+        )
+    dec_cols[part, cols] = dec_t[pl.ds(pl.multiple_of(me * fd + t * half, 16), half), :]
+    loads[1].wait()
+    loads[2].wait()
+
+    def consume(d):
+        r = rows(d, fd)
+        blk = x_all[r, :]
+        pre_acc[...] += dot(encv[r, :], blk, 0, 0)
+        skip_acc[...] += dot(swv[r, :], blk, 0, 0)
+
+    def line(yy, cc, use):
+        def body(k, carry):
+            use(at((z + nz - k) % nz, yy, cc))
+            return carry
+
+        lax.fori_loop(0, nz, body, 0)
+
+    line(y, c, consume)
+    gather_y(0, x_all, fd, to_other)
+    line(1 - y, c, consume)
+
+    def wait_consume(d):
+        arrived(x_all.at[rows(d, fd)], ag_recv.at[0, d])
+        consume(d)
+
+    line(y, 1 - c, wait_consume)
+    line(1 - y, 1 - c, wait_consume)
+
+    pre = pre_acc[...] + eb[...]
+    value, slope = gelu_pair(pre)
+    blocks = lax.broadcasted_iota(jnp.int32, pre.shape, 0) // BLK + me * (lat // BLK)
+    active = ids[0:1, :] == blocks
+    for r in range(1, ids.shape[0]):
+        active = active | (ids[r : r + 1, :] == blocks)
+    slope_s[...] = jnp.where(active, slope, 0.0)
+    code = jnp.where(active, value, 0.0).astype(bf16)
+    codes[rows(me, lat), :] = code
+
+    gather_own(1, codes, lat)
+    gather_z(1, codes, lat, nothing)
+    gather_y(1, codes, lat, nothing)
+    for k in range(1, n):
+        d = (me + k) % n
+        arrived(dec_cols.at[part, pl.ds(pl.multiple_of(d * lat, 128), lat)], dec_recv.at[d])
+    send(dec_cols.at[part], dec_cols.at[part], pair_send.at[1], pair_recv.at[1], xpeer)
+
+    def wait_code(d):
+        arrived(codes.at[rows(d, lat)], ag_recv.at[1, d])
+
+    line(y, 1 - c, wait_code)
+    line(1 - y, 1 - c, wait_code)
+    arrived(dec_cols.at[pl.ds(pl.multiple_of((1 - t) * half, 16), half)], pair_recv.at[1])
+    recon = dot(dec_cols[...], codes[...], 1, 0)
+    err = recon + skip_acc[...] + db[...] - tt[...].astype(f32)
+    go = (err * scale).astype(bf16)
+    go_all[rows(me, fd), :] = go
+    pre_acc[...] = jnp.zeros_like(pre_acc)
+
+    own_go = go_all.at[rows(me, fd)]
+    gather_own(2, go_all, fd)
+    send(own_go, go_oth, pair_send.at[2], pair_recv.at[2], xpeer)
+    gather_z(2, go_all, fd, nothing)
+
+    def back(d):
+        r = rows(d, fd)
+        blk = go_all[r, :]
+        pre_acc[...] += dot(dec_t[r, :], blk, 0, 0)
+        gd_part[r, :] = dot(blk, codes[rows(me, lat), :], 1, 1).astype(bf16)
+
+        @pl.when(d // nh == 1 - t)
+        def _():
+            j = d % nh
+            copy(
+                gd_part.at[r], gd_recv.at[rows(j, fd)], gd_send.at[j], gd_recv_sem.at[j], xpeer
+            ).start()
+
+    line(y, c, back)
+    gather_y(2, go_all, fd, nothing)
+    for zl in range(nz // 2):
+        for yy in range(2):
+            j = at(zl, yy, c)
+            blk = x_oth.at[rows(j, fd)]
+            arrived(blk, xo_recv.at[j])
+            send(blk, blk, xo_fwd.at[zl * 2 + yy], xo_recv.at[j], sib)
+    line(1 - y, c, back)
+
+    def wait_back(d):
+        arrived(go_all.at[rows(d, fd)], ag_recv.at[2, d])
+        back(d)
+
+    line(y, 1 - c, wait_back)
+    line(1 - y, 1 - c, wait_back)
+    dpre[...] = (pre_acc[...] * slope_s[...]).astype(bf16)
+    send(dpre, dpre_oth, pair_send.at[3], pair_recv.at[3], xpeer)
+
+    for zl in range(nz // 2):
+        for yy in range(2):
+            j = at(zl, yy, 1 - c)
+            arrived(x_oth.at[rows(j, fd)], xo_recv.at[j])
+    arrived(go_oth, pair_recv.at[2])
+
+    def skip_rows(j, carry):
+        r = rows(j, fd)
+        mine = x_all[rows(t * nh + j, fd), :]
+        gs[r, :] = dot(mine, go_all[rows(me, fd), :], 1, 1) + dot(x_oth[r, :], go_oth[...], 1, 1)
+        return carry
+
+    lax.fori_loop(0, nh, skip_rows, 0)
+    arrived(dpre_oth, pair_recv.at[3])
+
+    def enc_rows(j, carry):
+        r = rows(j, fd)
+        mine = x_all[rows(t * nh + j, fd), :]
+        ge[r, :] = dot(mine, dpre[...], 1, 1) + dot(x_oth[r, :], dpre_oth[...], 1, 1)
+        arrived(gd_recv.at[r], gd_recv_sem.at[j])
+        gd[r, :] = gd_part[rows(t * nh + j, fd), :].astype(f32) + gd_recv[r, :].astype(f32)
+        return carry
+
+    lax.fori_loop(0, nh, enc_rows, 0)
+    for cp in pending:
+        cp.wait_send()
+    for zl in range(nz // 2):
+        for yy in range(2):
+            j = at(zl, yy, c)
+            blk = x_oth.at[rows(j, fd)]
+            copy(blk, blk, xo_send.at[j], xo_recv.at[j], xpeer).wait_send()
+    for j in range(nh):
+        blk = gd_recv.at[rows(j, fd)]
+        copy(blk, blk, gd_send.at[j], gd_recv_sem.at[j], xpeer).wait_send()
+
+
+def fused(nz, inputs, target, enc_weight, enc_bias, dec_weight, dec_bias, skip_weight, block_ids):
+    tok, fd = inputs.shape
+    feat, lat = enc_weight.shape
+    n = 4 * nz
+    nh = n // 2
+    f32, bf16 = jnp.float32, jnp.bfloat16
+    vm, hbm = pl.BlockSpec(memory_space=pltpu.VMEM), pl.BlockSpec(memory_space=pl.ANY)
+    sem = pltpu.SemaphoreType.DMA
+    ge, gd, gs = pl.pallas_call(
+        functools.partial(fused_kernel, nz, 1.0 / math.sqrt(2 * tok)),
+        out_shape=(
+            jax.ShapeDtypeStruct((feat // 2, lat), f32),
+            jax.ShapeDtypeStruct((feat // 2, lat), f32),
+            jax.ShapeDtypeStruct((feat // 2, fd), f32),
+        ),
+        in_specs=[vm, vm, hbm, vm, hbm, vm, hbm, vm],
+        out_specs=(vm, vm, vm),
+        scratch_shapes=[
+            pltpu.VMEM((feat, lat), bf16),
+            pltpu.VMEM((lat, feat), bf16),
+            pltpu.VMEM((feat, fd), bf16),
+            pltpu.VMEM((feat, tok), bf16),
+            pltpu.VMEM((feat // 2, tok), bf16),
+            pltpu.VMEM((feat, lat), bf16),
+            pltpu.VMEM((fd, n * lat), bf16),
+            pltpu.VMEM((n * lat, tok), bf16),
+            pltpu.VMEM((feat, tok), bf16),
+            pltpu.VMEM((fd, tok), bf16),
+            pltpu.VMEM((feat, lat), bf16),
+            pltpu.VMEM((feat // 2, lat), bf16),
+            pltpu.VMEM((lat, tok), bf16),
+            pltpu.VMEM((lat, tok), bf16),
+            pltpu.VMEM((fd, tok), f32),
+            pltpu.VMEM((lat, tok), f32),
+            pltpu.VMEM((lat, tok), f32),
+            sem((3,)),
+            sem((3, 4 * nz)),
+            sem((3, n)),
+            sem((nh,)),
+            sem((nz,)),
+            sem((nh,)),
+            sem((n - 1,)),
+            sem((n,)),
+            sem((nh,)),
+            sem((nh,)),
+            sem((4,)),
+            sem((4,)),
+        ],
+        compiler_params=pltpu.CompilerParams(
+            collective_id=0, has_side_effects=True, vmem_limit_bytes=58 * 1024 * 1024
+        ),
+    )(
+        inputs.T, target.T, enc_weight, enc_bias[:, None], dec_weight, dec_bias[:, None],
+        skip_weight, block_ids.T,
+    )
+    return (ge, gd.T, gs)
 
 
 def local(
@@ -35,6 +344,12 @@
     owner = lax.axis_index("dict")
     n_dict = lax.axis_size("dict")
     n_tok = lax.axis_size("tok")
+    nz = n_dict // 4
+    aligned = tok_rows % 128 == 0 and feat_dev % 32 == 0 and lat_dev == 128
+    if n_tok == 2 and nz % 2 == 0 and nz * 4 == n_dict and aligned:
+        return fused(
+            nz, inputs, target, enc_weight, enc_bias, dec_weight, dec_bias, skip_weight, block_ids
+        )
     scale = 1.0 / math.sqrt(tok_rows * n_tok)
     f32, bf16 = jnp.float32, jnp.bfloat16
     blocks = (owner * lat_dev + jnp.arange(lat_dev, dtype=jnp.int32)) // BLK

time: 265 us -> 151 us (0.57)
  Pallas kernels: 0 us -> 135 us
  waiting for transfers between devices: 104 us -> 0 us
  blocking collectives: 83.6 us -> 0 us
  matrix products: 22.5 us -> 0 us
  local copies, waits for them, and re-layouts: 28.6 us -> 14.9 us
  between operations: 14 us -> 0.64 us
  other arithmetic: 7.65 us -> 0 us
  starting transfers between devices: 4.08 us -> 0 us
    pallas_call x0 -> x1, Pallas kernels: none -> 135 us  [fused(): pl.pallas_call(functools.partial(fused_kernel, nz, 1.0 / math.sqrt(2 * to...]
    all_to_all x2 -> x0, blocking collectives: 83.6 us -> none  [the longest x1 50.5 us: local(): lax.all_to_all(back.reshape(n_dict, lat_dev, tok_rows), 'dict', split_axi...]
    all_gather x2 -> x0, waiting for transfers between devices: 72 us -> none  [the longest x1 59.9 us: local(): whole = lax.all_gather(inputs, 'dict')]
    dot_general x7 -> x0, matrix products: 22.5 us -> none  [the longest x1 6.76 us: local(): jnp.einsum('btf,tm->bfm', whole, grad_out, preferred_element_type=f32)]
    reduce_scatter x3 -> x0, waiting for transfers between devices: 16.8 us -> none  [the longest x1 16.7 us: local(): lax.psum_scatter(enc_term, 'tok', scatter_dimension=0, tiled=True)]
    reshape x4 -> x0, local copies, waits for them, and re-layouts: 15.5 us -> none  [the longest x2 14.7 us: local(): skip_weight.reshape(n_dict, feat_dev, feat_dev)]
    all_to_all x1 -> x0, waiting for transfers between devices: 14.4 us -> none  [local(): lax.all_to_all(dec_weight.reshape(lat_dev, n_dict, feat_dev), 'dict', spl...]
    convert_element_type x3 -> x0, other arithmetic: 6.29 us -> none  [the longest x1 3 us: local(): lax.psum_scatter(skip_term, 'tok', scatter_dimension=0, tiled=True)]
  transfers between devices with their start and end apart: 6 -> 0, of which waited for: 4 -> 0; matrix products, arithmetic and copies ran while one was open for 17% -> 0% of each run, Pallas kernels for 0% -> 0%
where the time goes in v2:
time: 151 us; the launch traced here: 150 us
  Pallas kernels  135 us (89%)
  local copies, waits for them, and re-layouts  14.9 us (10%)
    pallas_call x1, Pallas kernels, fused(): pl.pallas_call(functools.partial(fused_kernel, nz, 1.0 / math.sqrt(2 * to...  135 us
    unnamed x6, local copies, waits for them, and re-layouts  12 us

profile of v2, /device:TPU:0, one launch (start us, length us, event | category | flops | bytes accessed | tf_op | source)
XLA Modules:
  0.0 150.3 jit_solution(15519771291126224519)
XLA Ops:
  0.6 1.4 copy.15.eb
  2.0 1.4 broadcast_in_dim.8.db
  3.5 4.7 %copy.17.sw = bf16[4608,288]{1,0:T(8,128)(2,1)} copy(bf16[4608,288]{0,1:T(8,128)(2,1)} %param.16) | data formatting | bytes 5308416 | tf_op args[6]
  8.2 134.8 %shard_map.103 = (f32[2304,128]{1,0:T(8,128)}, f32[2304,128]{1,0:T(8,128)}, f32[2304,288]{1,0:T(8,128)}) custom-call(bf16[288,512]{1,0:T(8,128)(2,1)} %bitcast.6, bf16[288,512]{1,0:T(8,128)(2,1)} %bitcast.7, bf16[4608,128]{1,0:T(8,128)(2,1)} %enc.1, f32[128,1]{1,0:T(8,128)} %copy.15.eb, bf16[128,4608]{1,0:T(8,128)(2,1)} %dec.1, ...), custom_call_target="tpu_custom_call" | custom-call | tf_op jit(solution)/shard_map/pallas_call | solution.py:280
  142.9 2.7 %copy.18 = f32[128,2304]{1,0:T(8,128)} copy(f32[128,2304]{0,1:T(8,128)} %bitcast.5) | data formatting | bytes 2359296
  145.6 0.0 copy-start
  145.6 3.7 %copy.19 = f32[2304,288]{0,1:T(8,128)} copy(f32[2304,288]{1,0:T(8,128)} %get-tuple-element.14) | data formatting | bytes 5308416
  149.3 0.0 copy-done
  149.3 1.0 copy.21
Async XLA Ops:
  145.6 3.7 %copy-start = (f32[2304,128]{1,0:T(8,128)S(1)}, f32[2304,128]{1,0:T(8,128)}, u32[]{:S(2)}) copy-start(f32[2304,128]{1,0:T(8,128)} %get-tuple-element.18) | copy-start | bytes 3538948

commit v3 on v2

--- a/solution.py
+++ b/solution.py
@@ -32,7 +32,7 @@
     ge, gd, gs,
     encv, decv, swv, x_all, x_oth, dec_t, dec_cols, codes, go_all, go_oth, gd_part, gd_recv,
     dpre, dpre_oth, skip_acc, pre_acc, slope_s,
-    load_sem, ag_send, ag_recv, xo_send, xo_fwd, xo_recv, dec_send, dec_recv, gd_send, gd_recv_sem,
+    gs_v, load_sem, up_send, down_send, y_send, sib_send, ag_recv, dx_send, dx_recv, xo_send, xo_fwd, xo_recv, dec_send, dec_recv, gd_send, gd_recv_sem,
     pair_send, pair_recv,
 ):
     f32, bf16 = jnp.float32, jnp.bfloat16
@@ -51,7 +51,6 @@
 
     sib, ypeer = (t, at(z, y, 1 - c)), (t, at(z, 1 - y, c))
     xpeer = (1 - t, me)
-    zs = [(z + k) % nz for k in range(nz)]
 
     def copy(src, dst, s, r, dev):
         return pltpu.make_async_remote_copy(
@@ -68,30 +67,80 @@
     def arrived(ref, r):
         copy(ref, ref, pair_send.at[0], r, xpeer).wait_recv()
 
+    def step(ref, s, r, dev):
+        copy(ref, ref, s, r, dev).start()
+
+    def pass_on(p, buf, size, zb):
+        d = at(zb, y, c)
+        blk = buf.at[rows(d, size)]
+        step(blk, y_send.at[p, zb], ag_recv.at[p, d], ypeer)
+        step(blk, sib_send.at[p, zb * 2 + y], ag_recv.at[p, d], sib)
+
+    def chain(p, buf, size, zb, up):
+        d = at(zb, y, c)
+        blk = buf.at[rows(d, size)]
+
+        @pl.when((z < nz - 1) if up else (z > 0))
+        def _():
+            to = (t, at(z + 1, y, c) if up else at(z - 1, y, c))
+            step(blk, (up_send if up else down_send).at[p, zb], ag_recv.at[p, d], to)
+
     def gather_own(p, buf, size):
-        own = buf.at[rows(me, size)]
-        for k in range(1, nz):
-            send(own, own, ag_send.at[p, k - 1], ag_recv.at[p, me], (t, at(zs[k], y, c)))
-        send(own, own, ag_send.at[p, nz - 1], ag_recv.at[p, me], ypeer)
-        send(own, own, ag_send.at[p, nz], ag_recv.at[p, me], sib)
-
-    def gather_z(p, buf, size, extra):
+        chain(p, buf, size, z, True)
+        chain(p, buf, size, z, False)
+        pass_on(p, buf, size, z)
+
+    def gather_z(p, buf, size, extra, between=lambda k: None):
         extra(me, z)
         for k in range(1, nz):
-            d = at(zs[nz - k], y, c)
+            for up in (True, False):
+                zb = z - k if up else z + k
+
+                @pl.when((zb >= 0) if up else (zb < nz))
+                def _():
+                    d = at(zb, y, c)
+                    arrived(buf.at[rows(d, size)], ag_recv.at[p, d])
+                    chain(p, buf, size, zb, up)
+                    pass_on(p, buf, size, zb)
+                    extra(d, zb)
+
+            between(k)
+
+    def gather_y(p, buf, size, extra):
+        def forward(zb):
+            d = at(zb, 1 - y, c)
             blk = buf.at[rows(d, size)]
             arrived(blk, ag_recv.at[p, d])
-            send(blk, blk, ag_send.at[p, nz + 2 * k - 1], ag_recv.at[p, d], ypeer)
-            send(blk, blk, ag_send.at[p, nz + 2 * k], ag_recv.at[p, d], sib)
-            extra(d, zs[nz - k])
-
-    def gather_y(p, buf, size, extra):
-        for k in range(nz):
-            d = at(zs[(nz - k) % nz], 1 - y, c)
-            blk = buf.at[rows(d, size)]
-            arrived(blk, ag_recv.at[p, d])
-            send(blk, blk, ag_send.at[p, 3 * nz - 1 + k], ag_recv.at[p, d], sib)
-            extra(d, zs[(nz - k) % nz])
+            step(blk, sib_send.at[p, zb * 2 + 1 - y], ag_recv.at[p, d], sib)
+            extra(d, zb)
+
+        forward(z)
+        for k in range(1, nz):
+            for up in (True, False):
+                zb = z - k if up else z + k
+
+                @pl.when((zb >= 0) if up else (zb < nz))
+                def _():
+                    forward(zb)
+
+    def drain(p, buf, size):
+        blk = buf.at[rows(me, size)]
+
+        def sent(s):
+            copy(blk, blk, s, ag_recv.at[p, me], sib).wait_send()
+
+        for zb in range(nz):
+            sent(y_send.at[p, zb])
+            sent(sib_send.at[p, zb * 2])
+            sent(sib_send.at[p, zb * 2 + 1])
+            if zb < nz - 1:
+                @pl.when((zb <= z) & (z < nz - 1))
+                def _():
+                    sent(up_send.at[p, zb])
+            if zb > 0:
+                @pl.when((zb >= z) & (z > 0))
+                def _():
+                    sent(down_send.at[p, zb])
 
     def nothing(d, zz):
         pass
@@ -107,7 +156,6 @@
     for cp in loads:
         cp.start()
     x_all[rows(me, fd), :] = xt[...]
-    skip_acc[...] = jnp.zeros_like(skip_acc)
     pre_acc[...] = jnp.zeros_like(pre_acc)
     pl.semaphore_wait(barrier, n)
 
@@ -140,13 +188,11 @@
         )
     dec_cols[part, cols] = dec_t[pl.ds(pl.multiple_of(me * fd + t * half, 16), half), :]
     loads[1].wait()
-    loads[2].wait()
 
     def consume(d):
         r = rows(d, fd)
         blk = x_all[r, :]
         pre_acc[...] += dot(encv[r, :], blk, 0, 0)
-        skip_acc[...] += dot(swv[r, :], blk, 0, 0)
 
     def line(yy, cc, use):
         def body(k, carry):
@@ -166,7 +212,14 @@
     line(y, 1 - c, wait_consume)
     line(1 - y, 1 - c, wait_consume)
 
-    pre = pre_acc[...] + eb[...]
+    def column(row):
+        size = row.shape[1]
+        eye = lax.broadcasted_iota(jnp.int32, (size, size), 0) == lax.broadcasted_iota(
+            jnp.int32, (size, size), 1
+        )
+        return jnp.sum(jnp.where(eye, row, 0.0), axis=1, keepdims=True)
+
+    pre = pre_acc[...] + column(eb[...])
     value, slope = gelu_pair(pre)
     blocks = lax.broadcasted_iota(jnp.int32, pre.shape, 0) // BLK + me * (lat // BLK)
     active = ids[0:1, :] == blocks
@@ -177,21 +230,38 @@
     codes[rows(me, lat), :] = code
 
     gather_own(1, codes, lat)
-    gather_z(1, codes, lat, nothing)
+    loads[2].wait()
+    wide = 512 if swv.shape[1] % 512 == 0 else 128
+    skip_acc[...] = column(db[...]) - tt[...].astype(f32)
+
+    def skip_cols(j, carry):
+        r = pl.ds(pl.multiple_of(j * wide, 128), wide)
+        skip_acc[...] += dot(swv[:, r], x_all[r, :], 1, 0)
+        return carry
+
+    lax.fori_loop(0, swv.shape[1] // wide, skip_cols, 0)
+
+    def dec_to_other(k):
+        if k == 1:
+            for i in range(n):
+                d = (me + i) % n
+                blk = dec_cols.at[part, pl.ds(pl.multiple_of(d * lat, 128), lat)]
+                if i:
+                    arrived(blk, dec_recv.at[d])
+                send(blk, blk, dx_send.at[i], dx_recv.at[d], xpeer)
+
+    gather_z(1, codes, lat, nothing, dec_to_other)
     gather_y(1, codes, lat, nothing)
-    for k in range(1, n):
-        d = (me + k) % n
-        arrived(dec_cols.at[part, pl.ds(pl.multiple_of(d * lat, 128), lat)], dec_recv.at[d])
-    send(dec_cols.at[part], dec_cols.at[part], pair_send.at[1], pair_recv.at[1], xpeer)
 
     def wait_code(d):
         arrived(codes.at[rows(d, lat)], ag_recv.at[1, d])
 
     line(y, 1 - c, wait_code)
     line(1 - y, 1 - c, wait_code)
-    arrived(dec_cols.at[pl.ds(pl.multiple_of((1 - t) * half, 16), half)], pair_recv.at[1])
-    recon = dot(dec_cols[...], codes[...], 1, 0)
-    err = recon + skip_acc[...] + db[...] - tt[...].astype(f32)
+    other = pl.ds(pl.multiple_of((1 - t) * half, 16), half)
+    for d in range(n):
+        arrived(dec_cols.at[other, d * lat : (d + 1) * lat], dx_recv.at[d])
+    err = dot(dec_cols[...], codes[...], 1, 0) + skip_acc[...]
     go = (err * scale).astype(bf16)
     go_all[rows(me, fd), :] = go
     pre_acc[...] = jnp.zeros_like(pre_acc)
@@ -199,7 +269,35 @@
     own_go = go_all.at[rows(me, fd)]
     gather_own(2, go_all, fd)
     send(own_go, go_oth, pair_send.at[2], pair_recv.at[2], xpeer)
-    gather_z(2, go_all, fd, nothing)
+    for zl in range(nz // 2):
+        for yy in range(2):
+            j = at(zl, yy, c)
+            blk = x_oth.at[rows(j, fd)]
+            arrived(blk, xo_recv.at[j])
+            send(blk, blk, xo_fwd.at[zl * 2 + yy], xo_recv.at[j], sib)
+    tall = 256 if gs_v.shape[1] % 256 == 0 else 128
+    gs_copy = pltpu.make_async_copy(gs_v, gs, load_sem.at[3])
+
+    def grad_skip(k):
+        if k == max(1, nz - 2):
+            for zl in range(nz // 2):
+                for yy in range(2):
+                    j = at(zl, yy, 1 - c)
+                    arrived(x_oth.at[rows(j, fd)], xo_recv.at[j])
+            arrived(go_oth, pair_recv.at[2])
+
+            def body(j, carry):
+                r = pl.ds(pl.multiple_of(j * tall, 128), tall)
+                mine = x_all[pl.ds(pl.multiple_of(t * nh * fd + j * tall, 16), tall), :]
+                gs_v[:, r] = dot(go_all[rows(me, fd), :], mine, 1, 1) + dot(
+                    go_oth[...], x_oth[r, :], 1, 1
+                )
+                return carry
+
+            lax.fori_loop(0, gs_v.shape[1] // tall, body, 0)
+            gs_copy.start()
+
+    gather_z(2, go_all, fd, nothing, grad_skip)
 
     def back(d):
         r = rows(d, fd)
@@ -216,12 +314,6 @@
 
     line(y, c, back)
     gather_y(2, go_all, fd, nothing)
-    for zl in range(nz // 2):
-        for yy in range(2):
-            j = at(zl, yy, c)
-            blk = x_oth.at[rows(j, fd)]
-            arrived(blk, xo_recv.at[j])
-            send(blk, blk, xo_fwd.at[zl * 2 + yy], xo_recv.at[j], sib)
     line(1 - y, c, back)
 
     def wait_back(d):
@@ -233,30 +325,27 @@
     dpre[...] = (pre_acc[...] * slope_s[...]).astype(bf16)
     send(dpre, dpre_oth, pair_send.at[3], pair_recv.at[3], xpeer)
 
-    for zl in range(nz // 2):
-        for yy in range(2):
-            j = at(zl, yy, 1 - c)
-            arrived(x_oth.at[rows(j, fd)], xo_recv.at[j])
-    arrived(go_oth, pair_recv.at[2])
-
-    def skip_rows(j, carry):
+
+    def dec_rows(j, carry):
         r = rows(j, fd)
-        mine = x_all[rows(t * nh + j, fd), :]
-        gs[r, :] = dot(mine, go_all[rows(me, fd), :], 1, 1) + dot(x_oth[r, :], go_oth[...], 1, 1)
+        arrived(gd_recv.at[r], gd_recv_sem.at[j])
+        gd[r, :] = gd_part[rows(t * nh + j, fd), :].astype(f32) + gd_recv[r, :].astype(f32)
         return carry
 
-    lax.fori_loop(0, nh, skip_rows, 0)
+    lax.fori_loop(0, nh, dec_rows, 0)
     arrived(dpre_oth, pair_recv.at[3])
 
     def enc_rows(j, carry):
         r = rows(j, fd)
         mine = x_all[rows(t * nh + j, fd), :]
         ge[r, :] = dot(mine, dpre[...], 1, 1) + dot(x_oth[r, :], dpre_oth[...], 1, 1)
-        arrived(gd_recv.at[r], gd_recv_sem.at[j])
-        gd[r, :] = gd_part[rows(t * nh + j, fd), :].astype(f32) + gd_recv[r, :].astype(f32)
         return carry
 
     lax.fori_loop(0, nh, enc_rows, 0)
+    gs_copy.wait()
+    drain(0, x_all, fd)
+    drain(1, codes, lat)
+    drain(2, go_all, fd)
     for cp in pending:
         cp.wait_send()
     for zl in range(nz // 2):
@@ -282,14 +371,14 @@
         out_shape=(
             jax.ShapeDtypeStruct((feat // 2, lat), f32),
             jax.ShapeDtypeStruct((feat // 2, lat), f32),
-            jax.ShapeDtypeStruct((feat // 2, fd), f32),
+            jax.ShapeDtypeStruct((fd, feat // 2), f32),
         ),
         in_specs=[vm, vm, hbm, vm, hbm, vm, hbm, vm],
-        out_specs=(vm, vm, vm),
+        out_specs=(vm, vm, hbm),
         scratch_shapes=[
             pltpu.VMEM((feat, lat), bf16),
             pltpu.VMEM((lat, feat), bf16),
-            pltpu.VMEM((feat, fd), bf16),
+            pltpu.VMEM((fd, feat), bf16),
             pltpu.VMEM((feat, tok), bf16),
             pltpu.VMEM((feat // 2, tok), bf16),
             pltpu.VMEM((feat, lat), bf16),
@@ -304,9 +393,15 @@
             pltpu.VMEM((fd, tok), f32),
             pltpu.VMEM((lat, tok), f32),
             pltpu.VMEM((lat, tok), f32),
-            sem((3,)),
-            sem((3, 4 * nz)),
+            pltpu.VMEM((fd, feat // 2), f32),
+            sem((4,)),
+            sem((3, nz)),
+            sem((3, nz)),
+            sem((3, nz)),
+            sem((3, 2 * nz)),
             sem((3, n)),
+            sem((n,)),
+            sem((n,)),
             sem((nh,)),
             sem((nz,)),
             sem((nh,)),
@@ -321,10 +416,10 @@
             collective_id=0, has_side_effects=True, vmem_limit_bytes=58 * 1024 * 1024
         ),
     )(
-        inputs.T, target.T, enc_weight, enc_bias[:, None], dec_weight, dec_bias[:, None],
-        skip_weight, block_ids.T,
+        inputs.T, target.T, enc_weight, enc_bias[None, :], dec_weight, dec_bias[None, :],
+        skip_weight.T, block_ids.T,
     )
-    return (ge, gd.T, gs)
+    return (ge, gd.T, gs.T)
 
 
 def local(
@@ -345,7 +440,7 @@
     n_dict = lax.axis_size("dict")
     n_tok = lax.axis_size("tok")
     nz = n_dict // 4
-    aligned = tok_rows % 128 == 0 and feat_dev % 32 == 0 and lat_dev == 128
+    aligned = tok_rows % 128 == 0 and enc_weight.shape[0] % 256 == 0 and feat_dev % 32 == 0 and lat_dev == 128
     if n_tok == 2 and nz % 2 == 0 and nz * 4 == n_dict and aligned:
         return fused(
             nz, inputs, target, enc_weight, enc_bias, dec_weight, dec_bias, skip_weight, block_ids

time: 151 us -> 124 us (0.82)
  Pallas kernels: 135 us -> 115 us
  local copies, waits for them, and re-layouts: 14.9 us -> 7.91 us
    pallas_call x1, Pallas kernels: 135 us -> 115 us  [fused(): pl.pallas_call(functools.partial(fused_kernel, nz, 1.0 / math.sqrt(2 * to...]
    unnamed x6 -> x5, local copies, waits for them, and re-layouts: 12 us -> 6.67 us
    broadcast_in_dim x2 -> x1, local copies, waits for them, and re-layouts: 2.84 us -> 1.25 us  [fused(): dec_bias[None, :]]
where the time goes in v3:
time: 124 us
  Pallas kernels  115 us (93%)
  local copies, waits for them, and re-layouts  7.91 us (6%)
    pallas_call x1, Pallas kernels, fused(): pl.pallas_call(functools.partial(fused_kernel, nz, 1.0 / math.sqrt(2 * to...  115 us
    unnamed x5, local copies, waits for them, and re-layouts  6.67 us

profile of v3, /device:TPU:0, one launch (start us, length us, event | category | flops | bytes accessed | tf_op | source)
XLA Modules:
  0.0 123.7 jit_solution(7313517693480808316)
XLA Ops:
  0.6 1.2 %broadcast_in_dim.7.db = f32[1,288]{1,0:T(1,128)} reshape(f32[288]{0:T(512)} %param.15) | data formatting | bytes 2304 | tf_op jit(solution)/shard_map/broadcast_in_dim | solution.py:419
  1.9 115.2 %shard_map.103 = (f32[2304,128]{1,0:T(8,128)}, f32[2304,128]{1,0:T(8,128)}, f32[288,2304]{1,0:T(8,128)}) custom-call(bf16[288,512]{1,0:T(8,128)(2,1)} %bitcast.10, bf16[288,512]{1,0:T(8,128)(2,1)} %bitcast.11, bf16[4608,128]{1,0:T(8,128)(2,1)} %enc.1, f32[1,128]{1,0:T(1,128)} %bitcast.13, bf16[128,4608]{1,0:T(8,128)(2,1)} %dec.1, ...), custom_call_target="tpu_custom_call" | custom-call | tf_op jit(solution)/shard_map/pallas_call | solution.py:369
  117.0 0.0 copy-start
  117.1 2.8 %copy.11 = f32[128,2304]{1,0:T(8,128)} copy(f32[128,2304]{0,1:T(8,128)} %bitcast.9) | data formatting | bytes 2359296
  119.9 2.4 %copy.14 = f32[2304,128]{1,0:T(8,128)} copy(f32[2304,128]{1,0:T(8,128)} %get-tuple-element.15) | data formatting | bytes 2359296
  122.2 0.0 copy-done
  122.2 1.5 %copy.15 = f32[2304,288]{0,1:T(8,128)} copy(f32[2304,288]{0,1:T(8,128)S(1)} %bitcast.8) | data formatting | bytes 5308416
Async XLA Ops:
  117.0 5.2 %copy-start = (f32[288,2304]{1,0:T(8,128)S(1)}, f32[288,2304]{1,0:T(8,128)}, u32[]{:S(2)}) copy-start(f32[288,2304]{1,0:T(8,128)} %get-tuple-element.8) | copy-start | bytes 7962628

commit v4 on v3

--- a/solution.py
+++ b/solution.py
@@ -90,38 +90,55 @@
         chain(p, buf, size, z, False)
         pass_on(p, buf, size, z)
 
-    def gather_z(p, buf, size, extra, between=lambda k: None):
-        extra(me, z)
-        for k in range(1, nz):
-            for up in (True, False):
-                zb = z - k if up else z + k
-
-                @pl.when((zb >= 0) if up else (zb < nz))
-                def _():
-                    d = at(zb, y, c)
-                    arrived(buf.at[rows(d, size)], ag_recv.at[p, d])
-                    chain(p, buf, size, zb, up)
-                    pass_on(p, buf, size, zb)
-                    extra(d, zb)
-
-            between(k)
-
-    def gather_y(p, buf, size, extra):
-        def forward(zb):
+    def at_step(k, use):
+        if k == 0:
+            use(z, True)
+            return
+        for up in (True, False):
+            zb = z - k if up else z + k
+
+            @pl.when((zb >= 0) if up else (zb < nz))
+            def _():
+                use(zb, up)
+
+    def gather(p, buf, size, extra, consume, between=lambda k: None):
+        def from_z(zb, up):
+            d = at(zb, y, c)
+            arrived(buf.at[rows(d, size)], ag_recv.at[p, d])
+            chain(p, buf, size, zb, up)
+            pass_on(p, buf, size, zb)
+            extra(d, zb)
+
+        def from_y(zb, up):
             d = at(zb, 1 - y, c)
             blk = buf.at[rows(d, size)]
             arrived(blk, ag_recv.at[p, d])
             step(blk, sib_send.at[p, zb * 2 + 1 - y], ag_recv.at[p, d], sib)
             extra(d, zb)
 
-        forward(z)
-        for k in range(1, nz):
-            for up in (True, False):
-                zb = z - k if up else z + k
-
-                @pl.when((zb >= 0) if up else (zb < nz))
-                def _():
-                    forward(zb)
+        def near(zb, up):
+            consume(at(zb, y, c))
+            other = at(zb, y, 1 - c)
+            arrived(buf.at[rows(other, size)], ag_recv.at[p, other])
+            consume(other)
+
+        def far(zb, up):
+            consume(at(zb, 1 - y, c))
+            other = at(zb, 1 - y, 1 - c)
+            arrived(buf.at[rows(other, size)], ag_recv.at[p, other])
+            consume(other)
+
+        extra(me, z)
+        for k in range(1, nz + 2):
+            if k < nz:
+                at_step(k, from_z)
+            if k <= nz:
+                at_step(k - 1, from_y)
+            between(k)
+            if k <= nz:
+                at_step(k - 1, near)
+            if k > 1:
+                at_step(k - 2, far)
 
     def drain(p, buf, size):
         blk = buf.at[rows(me, size)]
@@ -173,20 +190,23 @@
                 x_all.at[rows(d, fd)], x_oth.at[rows(j, fd)], xo_send.at[j], xo_recv.at[j], xpeer
             ).start()
 
-    gather_z(0, x_all, fd, to_other)
-
     cols = pl.ds(pl.multiple_of(me * lat, 128), lat)
     part = pl.ds(pl.multiple_of(t * half, 16), half)
-    for k in range(1, n):
-        d = (me + k) % n
-        send(
-            dec_t.at[pl.ds(pl.multiple_of(d * fd + t * half, 16), half)],
-            dec_cols.at[part, cols],
-            dec_send.at[k - 1],
-            dec_recv.at[me],
-            (t, d),
-        )
-    dec_cols[part, cols] = dec_t[pl.ds(pl.multiple_of(me * fd + t * half, 16), half), :]
+
+    def dec_columns(k):
+        if k != max(1, nz - 2):
+            return
+        for i in range(1, n):
+            d = (me + i) % n
+            send(
+                dec_t.at[pl.ds(pl.multiple_of(d * fd + t * half, 16), half)],
+                dec_cols.at[part, cols],
+                dec_send.at[i - 1],
+                dec_recv.at[me],
+                (t, d),
+            )
+        dec_cols[part, cols] = dec_t[pl.ds(pl.multiple_of(me * fd + t * half, 16), half), :]
+
     loads[1].wait()
 
     def consume(d):
@@ -194,23 +214,7 @@
         blk = x_all[r, :]
         pre_acc[...] += dot(encv[r, :], blk, 0, 0)
 
-    def line(yy, cc, use):
-        def body(k, carry):
-            use(at((z + nz - k) % nz, yy, cc))
-            return carry
-
-        lax.fori_loop(0, nz, body, 0)
-
-    line(y, c, consume)
-    gather_y(0, x_all, fd, to_other)
-    line(1 - y, c, consume)
-
-    def wait_consume(d):
-        arrived(x_all.at[rows(d, fd)], ag_recv.at[0, d])
-        consume(d)
-
-    line(y, 1 - c, wait_consume)
-    line(1 - y, 1 - c, wait_consume)
+    gather(0, x_all, fd, to_other, consume, dec_columns)
 
     def column(row):
         size = row.shape[1]
@@ -250,14 +254,7 @@
                     arrived(blk, dec_recv.at[d])
                 send(blk, blk, dx_send.at[i], dx_recv.at[d], xpeer)
 
-    gather_z(1, codes, lat, nothing, dec_to_other)
-    gather_y(1, codes, lat, nothing)
-
-    def wait_code(d):
-        arrived(codes.at[rows(d, lat)], ag_recv.at[1, d])
-
-    line(y, 1 - c, wait_code)
-    line(1 - y, 1 - c, wait_code)
+    gather(1, codes, lat, nothing, lambda d: None, dec_to_other)
     other = pl.ds(pl.multiple_of((1 - t) * half, 16), half)
     for d in range(n):
         arrived(dec_cols.at[other, d * lat : (d + 1) * lat], dx_recv.at[d])
@@ -297,8 +294,6 @@
             lax.fori_loop(0, gs_v.shape[1] // tall, body, 0)
             gs_copy.start()
 
-    gather_z(2, go_all, fd, nothing, grad_skip)
-
     def back(d):
         r = rows(d, fd)
         blk = go_all[r, :]
@@ -312,27 +307,22 @@
                 gd_part.at[r], gd_recv.at[rows(j, fd)], gd_send.at[j], gd_recv_sem.at[j], xpeer
             ).start()
 
-    line(y, c, back)
-    gather_y(2, go_all, fd, nothing)
-    line(1 - y, c, back)
-
-    def wait_back(d):
-        arrived(go_all.at[rows(d, fd)], ag_recv.at[2, d])
-        back(d)
-
-    line(y, 1 - c, wait_back)
-    line(1 - y, 1 - c, wait_back)
+    gather(2, go_all, fd, nothing, back, grad_skip)
     dpre[...] = (pre_acc[...] * slope_s[...]).astype(bf16)
     send(dpre, dpre_oth, pair_send.at[3], pair_recv.at[3], xpeer)
 
 
+    for j in range(nh):
+        arrived(gd_recv.at[rows(j, fd)], gd_recv_sem.at[j])
+
     def dec_rows(j, carry):
-        r = rows(j, fd)
-        arrived(gd_recv.at[r], gd_recv_sem.at[j])
-        gd[r, :] = gd_part[rows(t * nh + j, fd), :].astype(f32) + gd_recv[r, :].astype(f32)
+        r = rows(j, lat)
+        mine = gd_part[pl.ds(pl.multiple_of(t * nh * fd + j * lat, 16), lat), :]
+        total = mine.astype(f32) + gd_recv[r, :].astype(f32)
+        gd[:, pl.ds(pl.multiple_of(j * lat, 128), lat)] = total.T
         return carry
 
-    lax.fori_loop(0, nh, dec_rows, 0)
+    lax.fori_loop(0, nh * fd // lat, dec_rows, 0)
     arrived(dpre_oth, pair_recv.at[3])
 
     def enc_rows(j, carry):
@@ -370,7 +360,7 @@
         functools.partial(fused_kernel, nz, 1.0 / math.sqrt(2 * tok)),
         out_shape=(
             jax.ShapeDtypeStruct((feat // 2, lat), f32),
-            jax.ShapeDtypeStruct((feat // 2, lat), f32),
+            jax.ShapeDtypeStruct((lat, feat // 2), f32),
             jax.ShapeDtypeStruct((fd, feat // 2), f32),
         ),
         in_specs=[vm, vm, hbm, vm, hbm, vm, hbm, vm],
@@ -419,7 +409,7 @@
         inputs.T, target.T, enc_weight, enc_bias[None, :], dec_weight, dec_bias[None, :],
         skip_weight.T, block_ids.T,
     )
-    return (ge, gd.T, gs.T)
+    return (ge, gd, gs.T)
 
 
 def local(

time: 124 us -> 123 us (level)
  the two profiles are of different devices: /device:TPU:0 before, /device:TPU:6 now
where the time goes in v4:
time: 123 us; the launch traced here: 122 us
  Pallas kernels  114 us (93%)
  local copies, waits for them, and re-layouts  7.62 us (6%)
    pallas_call x1, Pallas kernels, fused(): pl.pallas_call(functools.partial(fused_kernel, nz, 1.0 / math.sqrt(2 * to...  114 us
    unnamed x5, local copies, waits for them, and re-layouts  6.37 us

profile of v4, /device:TPU:6, one launch (start us, length us, event | category | flops | bytes accessed | tf_op | source)
XLA Modules:
  0.0 122.5 jit_solution(7551515117418452309)
XLA Ops:
  0.6 1.2 %broadcast_in_dim.7.db = f32[1,288]{1,0:T(1,128)} reshape(f32[288]{0:T(512)} %param.15) | data formatting | bytes 2304 | tf_op jit(solution)/shard_map/broadcast_in_dim | solution.py:409
  1.9 114.2 %shard_map.103 = (f32[2304,128]{1,0:T(8,128)}, f32[128,2304]{1,0:T(8,128)}, f32[288,2304]{1,0:T(8,128)}) custom-call(bf16[288,512]{1,0:T(8,128)(2,1)} %bitcast.8, bf16[288,512]{1,0:T(8,128)(2,1)} %bitcast.9, bf16[4608,128]{1,0:T(8,128)(2,1)} %enc.1, f32[1,128]{1,0:T(1,128)} %bitcast.11, bf16[128,4608]{1,0:T(8,128)(2,1)} %dec.1, ...), custom_call_target="tpu_custom_call" | custom-call | tf_op jit(solution)/shard_map/pallas_call | solution.py:359
  116.1 0.0 copy-start
  116.1 2.5 %copy.14 = f32[2304,128]{1,0:T(8,128)} copy(f32[2304,128]{1,0:T(8,128)} %get-tuple-element.12) | data formatting | bytes 2359296
  118.6 2.4 %copy.15 = f32[128,2304]{1,0:T(8,128)} copy(f32[128,2304]{1,0:T(8,128)} %get-tuple-element.13) | data formatting | bytes 2359296
  121.0 0.0 copy-done
  121.0 1.5 %copy.16 = f32[2304,288]{0,1:T(8,128)} copy(f32[2304,288]{0,1:T(8,128)S(1)} %bitcast.7) | data formatting | bytes 5308416
Async XLA Ops:
  116.1 4.9 %copy-start = (f32[288,2304]{1,0:T(8,128)S(1)}, f32[288,2304]{1,0:T(8,128)}, u32[]{:S(2)}) copy-start(f32[288,2304]{1,0:T(8,128)} %get-tuple-element.8) | copy-start | bytes 7962628

commit v5 on v4

--- a/solution.py
+++ b/solution.py
@@ -194,7 +194,7 @@
     part = pl.ds(pl.multiple_of(t * half, 16), half)
 
     def dec_columns(k):
-        if k != max(1, nz - 2):
+        if k != max(1, nz - 1):
             return
         for i in range(1, n):
             d = (me + i) % n

time: 123 us -> 122 us (level)
  the two profiles are of different devices: /device:TPU:6 before, /device:TPU:24 now
where the time goes in v5:
time: 122 us
  Pallas kernels  114 us (93%)
  local copies, waits for them, and re-layouts  7.62 us (6%)
    pallas_call x1, Pallas kernels, fused(): pl.pallas_call(functools.partial(fused_kernel, nz, 1.0 / math.sqrt(2 * to...  114 us
    unnamed x5, local copies, waits for them, and re-layouts  6.37 us

profile of v5, /device:TPU:24, one launch (start us, length us, event | category | flops | bytes accessed | tf_op | source)
XLA Modules:
  0.0 122.0 jit_solution(17068001785404456439)
XLA Ops:
  0.6 1.2 %broadcast_in_dim.7.db = f32[1,288]{1,0:T(1,128)} reshape(f32[288]{0:T(512)} %param.15) | data formatting | bytes 2304 | tf_op jit(solution)/shard_map/broadcast_in_dim | solution.py:409
  1.9 113.8 %shard_map.103 = (f32[2304,128]{1,0:T(8,128)}, f32[128,2304]{1,0:T(8,128)}, f32[288,2304]{1,0:T(8,128)}) custom-call(bf16[288,512]{1,0:T(8,128)(2,1)} %bitcast.8, bf16[288,512]{1,0:T(8,128)(2,1)} %bitcast.9, bf16[4608,128]{1,0:T(8,128)(2,1)} %enc.1, f32[1,128]{1,0:T(1,128)} %bitcast.11, bf16[128,4608]{1,0:T(8,128)(2,1)} %dec.1, ...), custom_call_target="tpu_custom_call" | custom-call | tf_op jit(solution)/shard_map/pallas_call | solution.py:359
  115.7 0.0 copy-start
  115.7 2.5 %copy.14 = f32[2304,128]{1,0:T(8,128)} copy(f32[2304,128]{1,0:T(8,128)} %get-tuple-element.12) | data formatting | bytes 2359296
  118.2 2.4 %copy.15 = f32[128,2304]{1,0:T(8,128)} copy(f32[128,2304]{1,0:T(8,128)} %get-tuple-element.13) | data formatting | bytes 2359296
  120.5 0.0 copy-done
  120.5 1.5 %copy.16 = f32[2304,288]{0,1:T(8,128)} copy(f32[2304,288]{0,1:T(8,128)S(1)} %bitcast.7) | data formatting | bytes 5308416
Async XLA Ops:
  115.7 4.9 %copy-start = (f32[288,2304]{1,0:T(8,128)S(1)}, f32[288,2304]{1,0:T(8,128)}, u32[]{:S(2)}) copy-start(f32[288,2304]{1,0:T(8,128)} %get-tuple-element.8) | copy-start | bytes 7962628
